TPU v7x, 256 devices: a whole 4x4x8 slice. The times are simulated.
256 devices in a mesh: seq: 32 (over z, x), exp: 8 (over y, core).
Axes of the slice: x: 4, y: 4, z: 8, core: 2. Of those that a mesh axis runs over, the one named last changes fastest.
Arguments:
- mixer_input: bfloat16 [2048, 8192], P('seq', 'exp'), may hold values from -6 to 6
- gate_input: bfloat16 [2048, 8192], P('seq', 'exp'), may hold values from -6 to 6
- conv_weight: bfloat16 [4, 8192], P(None, 'exp'), may hold values from -3 to 3
- conv_bias: float32 [8192], P('exp'), may hold values from -3 to 3
- rank_weight: bfloat16 [8192, 256], P('exp'), may hold values from -0.0625 to 0.0625
- state_weight: bfloat16 [8192, 32], P('exp'), may hold values from -0.03125 to 0.03125
- delta_weight: bfloat16 [256, 8192], P(None, 'exp'), may hold values from -0.375 to 0.375
- delta_bias: float32 [8192], P('exp'), may hold values from -1 to 1
- log_rates: float32 [16, 8192], P(None, 'exp'), may hold values from -10 to -1
- skip_gain: float32 [8192], P('exp'), may hold values from 0.5 to 1.5
- out_proj: bfloat16 [8192, 4096], P('exp', 'seq'), may hold values from -0.0625 to 0.0625
- residual: bfloat16 [2048, 4096], P(('seq', 'exp')), may hold values from -3 to 3
- norm_gain: float32 [4096], replicated, may hold values from 0.5 to 1.5
- router: float32 [4096, 8], replicated, may hold values from -0.09375 to 0.09375
- w_gate: bfloat16 [8, 4096, 14336], P('exp', None, 'seq'), may hold values from -0.09375 to 0.09375
- w_up: bfloat16 [8, 4096, 14336], P('exp', None, 'seq'), may hold values from -0.09375 to 0.09375
- w_down: bfloat16 [8, 14336, 4096], P('exp', 'seq'), may hold values from -0.09375 to 0.09375
- routes: int32 [2048, 2], P(('seq', 'exp')), may hold values from 0 to 7, all different within a row; in each aligned block of 8 rows (0 to 7, 8 to 15, ...) at most 4 rows name the same one
Outputs:
- layer_out: bfloat16 [2048, 4096], P(('seq', 'exp'))
- expert_mix: float32 [2048, 4096], P(('seq', 'exp'))
Inputs may be any that keep to these rules, and one draw needn't show every extreme that they name: `routes`: each row names two different experts; among the 8 rows of one device no expert is named more than 4 times, a bound that some block reaches there on some device.
All inputs are finite; a program needn't handle non-finite values.
Results may differ from a plain program's by a relative error of at most 0.024.
Values may be sent and summed in bfloat16 or wider, within the bound.
No kernel may reach another device: no remote copies, remote signals or barrier semaphores. Data moves between devices by JAX's collectives and lax.ppermute only.
A program may use at most 128 MiB of HBM per device.

v0:
```python
import jax
import jax.numpy as jnp
from jax import lax
from jax.sharding import PartitionSpec as P


def shifted(block, axis, distance):
    devices = range(lax.axis_size(axis))
    route = [(i - distance, i) for i in devices if i - distance in devices]
    return lax.ppermute(block, axis, route)


def entering(array, axis, combine, identity):
    count, index = (lax.axis_size(axis), lax.axis_index(axis))
    everything = jax.tree.map(lambda part: lax.all_gather(part, axis), array)
    start = jax.tree.map(
        lambda part, zero: jnp.broadcast_to(jnp.asarray(zero, part.dtype), part.shape),
        array,
        identity,
    )

    def hop(k, before):
        reached = k < index
        new = combine(before, jax.tree.map(lambda part: part[k], everything))
        return jax.tree.map(lambda a, b: jnp.where(reached, a, b), new, before)

    return lax.fori_loop(0, count, hop, start)


def combine_pair(earlier, following):
    return (earlier[0] * following[0], following[0] * earlier[1] + following[1])


def body(
    mixer_input,
    gate_input,
    conv_weight,
    conv_bias,
    rank_weight,
    state_weight,
    delta_weight,
    delta_bias,
    log_rates,
    skip_gain,
    out_proj,
    residual,
    norm_gain,
    router,
    w_gate,
    w_up,
    w_down,
    routes,
):
    taps = conv_weight.shape[0]
    block_rows = mixer_input.shape[0]
    rim_rows = shifted(mixer_input[block_rows - (taps - 1) :], "seq", 1)
    padded = jnp.concatenate([rim_rows, mixer_input], axis=0)
    conv_sum = jnp.zeros(mixer_input.shape, jnp.float32) + conv_bias[None, :]
    for offset in range(taps):
        conv_sum = conv_sum + conv_weight[offset].astype(jnp.float32)[None, :] * padded[
            offset : offset + block_rows
        ].astype(jnp.float32)
    conv_act = jax.nn.silu(conv_sum).astype(jnp.bfloat16)
    delta_part = jnp.dot(conv_act, rank_weight, preferred_element_type=jnp.float32)
    state_part = jnp.dot(conv_act, state_weight, preferred_element_type=jnp.float32)
    delta_sum, state_maps = lax.psum((delta_part, state_part), "exp")
    delta_low = delta_sum.astype(jnp.bfloat16)
    states = log_rates.shape[0]
    input_map = state_maps[:, :states]
    output_map = state_maps[:, states:]
    delta = jax.nn.softplus(
        jnp.dot(delta_low, delta_weight, preferred_element_type=jnp.float32) + delta_bias[None, :]
    )
    decay_rate = jnp.exp(log_rates)
    conv_float = conv_act.astype(jnp.float32)
    driven = (delta * conv_float)[:, None, :] * input_map[:, :, None]
    decays = jnp.exp(-delta[:, None, :] * decay_rate[None])
    passed = jnp.cumsum(delta, axis=0)
    total_dt = passed[-1]
    weights_left = jnp.exp(-(total_dt[None, :] - passed)[:, None, :] * decay_rate[None])
    transform = (jnp.exp(-total_dt[None, :] * decay_rate), jnp.sum(weights_left * driven, axis=0))
    incoming = entering(
        transform, "seq", combine_pair, (jnp.ones_like(decay_rate), jnp.zeros_like(decay_rate))
    )
    start_state = incoming[1]

    def advance(carried, inputs):
        decay_t, driven_t, output_t = inputs
        carried = decay_t * carried + driven_t
        return (carried, jnp.sum(output_t[:, None] * carried, axis=0))

    last_state, scan_out = lax.scan(advance, start_state, (decays, driven, output_map))
    scan_out = scan_out + skip_gain[None, :] * conv_float
    gated = (scan_out * jax.nn.silu(gate_input.astype(jnp.float32))).astype(jnp.bfloat16)
    tok_dev = residual.shape[0]
    partial_value = jnp.dot(
        gated,
        lax.all_gather(out_proj, "seq", axis=1, tiled=True),
        preferred_element_type=jnp.float32,
    )
    mamba_out = lax.psum_scatter(partial_value, "exp", scatter_dimension=0, tiled=True)
    hidden = residual.astype(jnp.float32) + mamba_out
    mean_square = jnp.mean(hidden * hidden, axis=1, keepdims=True)
    normed = (hidden * lax.rsqrt(mean_square + 1e-05) * norm_gain[None, :]).astype(jnp.bfloat16)
    logits = jnp.dot(normed.astype(jnp.float32), router, precision=lax.Precision.HIGHEST)
    experts = router.shape[1]
    expert_ids = jnp.arange(experts, dtype=jnp.int32)
    matches = (routes[:, :, None] == expert_ids[None, None, :]).astype(jnp.float32)
    chosen = jnp.sum(matches * logits[:, None, :], axis=2)
    route_weights = jax.nn.sigmoid(chosen - chosen[:, ::-1])
    capacity = max(2, 4 * tok_dev // experts)
    flat_ids = routes.reshape(-1)
    route_pos = jnp.arange(flat_ids.shape[0], dtype=jnp.int32)
    earlier_same = (flat_ids[:, None] == flat_ids[None, :]) & (
        route_pos[None, :] < route_pos[:, None]
    )
    slot_rank = jnp.sum(earlier_same.astype(jnp.int32), axis=1)
    slot_of = flat_ids * capacity + slot_rank
    slot_ids = jnp.arange(experts * capacity, dtype=jnp.int32)
    placing = (slot_ids[:, None] == slot_of[None, :]).astype(jnp.bfloat16)
    repeated = jnp.repeat(normed, 2, axis=0)
    outbound = jnp.dot(placing, repeated, preferred_element_type=jnp.float32).astype(jnp.bfloat16)
    arrived = lax.all_to_all(outbound, "exp", split_axis=0, concat_axis=0, tiled=True)
    gate_local = w_gate[0]
    up_local = w_up[0]
    down_local = w_down[0]
    shard_part = lax.all_gather(arrived, "seq", axis=0, tiled=True)
    gate_part = jnp.dot(shard_part, gate_local, preferred_element_type=jnp.float32)
    up_part = jnp.dot(shard_part, up_local, preferred_element_type=jnp.float32)
    activated = (jax.nn.silu(gate_part) * up_part).astype(jnp.bfloat16)
    expert_out = lax.psum_scatter(
        jnp.dot(activated, down_local, preferred_element_type=jnp.float32).astype(jnp.bfloat16),
        "seq",
        scatter_dimension=0,
        tiled=True,
    ).astype(jnp.float32)
    returned = lax.all_to_all(expert_out, "exp", split_axis=0, concat_axis=0, tiled=True)
    picked = jnp.take(returned, slot_of, axis=0)
    moe_sum = jnp.sum(picked.reshape(tok_dev, 2, -1) * route_weights[:, :, None], axis=1)
    return ((hidden + moe_sum).astype(jnp.bfloat16), moe_sum)


def solution(mesh):
    in_specs = (
        P("seq", "exp"),
        P("seq", "exp"),
        P(None, "exp"),
        P("exp"),
        P("exp", None),
        P("exp", None),
        P(None, "exp"),
        P("exp"),
        P(None, "exp"),
        P("exp"),
        P("exp", "seq"),
        P(("seq", "exp"), None),
        P(),
        P(),
        P("exp", None, "seq"),
        P("exp", None, "seq"),
        P("exp", "seq", None),
        P(("seq", "exp"), None),
    )
    out_specs = (P(("seq", "exp"), None), P(("seq", "exp"), None))
    return jax.shard_map(body, mesh=mesh, in_specs=in_specs, out_specs=out_specs, check_vma=False)
```

profile of v0, /device:TPU:1, one launch (start us, length us, event | category | flops | bytes accessed | tf_op | source)
XLA Modules:
  0.0 738.1 jit_solution(16103797339628601987)
XLA Ops:
  8.0 3.9 collective-permute-start
  12.8 1.4 multiply_convert_fusion.1
  14.2 1.2 fusion.34
  15.4 1.0 fusion.35
  16.4 23.9 %all-reduce = (bf16[64,256]{1,0:T(8,128)(2,1)S(1)}, f32[64,32]{0,1:T(8,128)S(1)}) all-reduce(f32[64,256]{1,0:T(8,128)S(1)} %fusion.34, f32[64,32]{0,1:T(8,128)S(1)} %fusion.35), channel_id=1, replica_groups=mesh['seq'=32,'exp'=8] {'exp'}, use_global_device_ids=true, to_apply=%region_0.1 | all-reduce | flops 18432 | bytes 114688 | tf_op jit(solution)/shard_map/psum | solution.py:66
  40.3 1.0 fusion.30
  41.7 1.5 fusion.32
  43.2 4.3 broadcast_multiply_fusion
  49.2 77.0 %all-gather.13.cloned.1.call-done = f32[512,1024]{1,0:T(8,128)} async-done(((f32[16,1024]{1,0:T(8,128)}), f32[512,1024]{1,0:T(8,128)}) %all-gather.13.cloned.1.call-update) | async-done | bytes 2097168 | tf_op jit(solution)/shard_map/all_gather | solution.py:15
  126.2 78.3 %all-gather.11.cloned.1.call-done = f32[512,1024]{1,0:T(8,128)} async-done(((f32[16,1024]{1,0:T(8,128)}), f32[512,1024]{1,0:T(8,128)}) %all-gather.11.cloned.1.call-update) | async-done | bytes 2097168 | tf_op jit(solution)/shard_map/all_gather | solution.py:15
  204.5 30.0 %while.29 = (s32[]{:T(128)}, f32[16,1024]{1,0:T(8,128)S(1)}, s32[]{:T(128)}, f32[32,16,1024]{2,1,0:T(8,128)}, f32[32,16,1024]{2,1,0:T(8,128)}) while((s32[]{:T(128)}, f32[16,1024]{1,0:T(8,128)S(1)}, s32[]{:T(128)}, f32[32,16,1024]{2,1,0:T(8,128)}, f32[32,16,1024]{2,1,0:T(8,128)}) %tuple.91), condition=%wide.region_5.6_spmd.clone.clone, body=%wide.region_4.5_spmd.clone.sunk.clone | while | flops 65540 | bytes 262229 | solution.py:27
  234.5 71.4 %while.28 = (s32[]{:T(128)}, f32[16,1024]{1,0:T(8,128)S(1)}, f32[64,1024]{1,0:T(8,128)S(1)}, f32[64,16,1024]{2,1,0:T(8,128)}, f32[64,16,1024]{2,1,0:T(8,128)}, /*index=5*/f32[64,16]{1,0:T(8,128)S(1)}) while((s32[]{:T(128)}, f32[16,1024]{1,0:T(8,128)S(1)}, f32[64,1024]{1,0:T(8,128)S(1)}, f32[64,16,1024]{2,1,0:T(8,128)}, ...), condition=%wide.region_8.9_spmd.clone, body=%wide.region_6.8_spmd.sunk.clone | while | flops 64514 | bytes 274705 | solution.py:92
  234.5 1.0 multiply_reduce_fusion.6
  236.8 1.0 multiply_reduce_fusion.6
  237.9 1.0 multiply_reduce_fusion.6
  239.0 1.0 multiply_reduce_fusion.6
  240.1 1.0 multiply_reduce_fusion.6
  241.2 1.0 multiply_reduce_fusion.6
  242.4 1.0 multiply_reduce_fusion.6
  243.5 1.0 multiply_reduce_fusion.6
  244.6 1.0 multiply_reduce_fusion.6
  245.7 1.0 multiply_reduce_fusion.6
  246.8 1.0 multiply_reduce_fusion.6
  247.9 1.0 multiply_reduce_fusion.6
  249.0 1.0 multiply_reduce_fusion.6
  250.2 1.0 multiply_reduce_fusion.6
  260.2 1.0 multiply_reduce_fusion.6
  261.3 1.0 multiply_reduce_fusion.6
  262.4 1.0 multiply_reduce_fusion.6
  263.5 1.0 multiply_reduce_fusion.6
  264.7 1.0 multiply_reduce_fusion.6
  270.2 1.0 multiply_reduce_fusion.6
  271.4 1.0 multiply_reduce_fusion.6
  274.7 1.0 multiply_reduce_fusion.6
  275.8 1.0 multiply_reduce_fusion.6
  276.9 1.0 multiply_reduce_fusion.6
  278.1 1.0 multiply_reduce_fusion.6
  279.2 1.0 multiply_reduce_fusion.6
  284.8 1.0 multiply_reduce_fusion.6
  285.9 1.0 multiply_reduce_fusion.6
  287.0 1.0 multiply_reduce_fusion.6
  288.1 1.0 multiply_reduce_fusion.6
  289.2 1.0 multiply_reduce_fusion.6
  290.4 1.0 multiply_reduce_fusion.6
  291.5 1.0 multiply_reduce_fusion.6
  292.6 1.0 multiply_reduce_fusion.6
  293.7 1.0 multiply_reduce_fusion.6
  298.2 1.0 multiply_reduce_fusion.6
  299.3 1.0 multiply_reduce_fusion.6
  300.4 1.0 multiply_reduce_fusion.6
  304.9 1.0 multiply_reduce_fusion.6
  306.0 3.2 all-gather.7.cloned.1.call-done
  309.2 6.1 fusion.20
  315.7 32.0 %reduce-scatter.3.cloned.1.call-done = f32[8,4096]{1,0:T(8,128)} async-done(((f32[64,4096]{1,0:T(8,128)}), f32[8,4096]{1,0:T(8,128)}) %reduce-scatter.3.cloned.1.call-update) | async-done | bytes 131088 | tf_op jit(solution)/shard_map/reduce_scatter | solution.py:101
  347.7 1.1 multiply_reduce_fusion.3
  348.8 1.0 multiply_convert_fusion.2
  350.2 12.0 %all_to_all.28 = bf16[8,4,4096]{2,1,0:T(4,128)(2,1)S(1)} all-to-all(bf16[8,4,4096]{2,1,0:T(4,128)(2,1)S(1)} %all_to_all.18), channel_id=1, replica_groups=mesh['seq'=32,'exp'=8] {'exp'}, dimensions={0} | all-to-all | bytes 524288 | tf_op jit(solution)/shard_map/all_to_all | solution.py:123
  363.3 97.7 %all-gather.9.cloned.1.call-done = bf16[1024,4096]{1,0:T(8,128)(2,1)} async-done(((bf16[32,4096]{1,0:T(8,128)(2,1)}), bf16[1024,4096]{1,0:T(8,128)(2,1)}) %all-gather.9.cloned.1.call-update) | async-done | bytes 8388624 | tf_op jit(solution)/shard_map/all_gather | solution.py:127
  460.9 9.7 %fusion.5 = f32[1024,448]{0,1:T(8,128)} fusion(bf16[1024,4096]{1,0:T(8,128)(2,1)} %all-gather.9.cloned.1.call-done, bf16[1,4096,448]{1,2,0:T(8,128)(2,1)} %param.36), kind=kOutput, calls=%fused_computation.16 | convolution fusion | flops 3758096384 | bytes 13893632 | tf_op jit(solution)/shard_map/dot_general | solution.py:128
  470.6 15.4 %convolution_convert_fusion = bf16[1024,4096]{1,0:T(8,128)(2,1)} fusion(bf16[1,448,4096]{2,1,0:T(8,128)(2,1)} %param.38, f32[1024,448]{0,1:T(8,128)} %fusion.5, bf16[1024,4096]{1,0:T(8,128)(2,1)} %all-gather.9.cloned.1.call-done, bf16[1,4096,448]{1,2,0:T(8,128)(2,1)} %param.37), kind=kOutput, calls=%fused_computation.9 | convolution fusion | flops 7523139584 | bytes 25952256 | tf_op jit(solution)/shard_map/dot_general | solution.py:132
  486.3 222.6 %reduce-scatter.5.cloned.1.call-done = bf16[32,4096]{1,0:T(8,128)(2,1)} async-done(((bf16[1024,4096]{1,0:T(8,128)(2,1)}), bf16[32,4096]{1,0:T(8,128)(2,1)}) %reduce-scatter.5.cloned.1.call-update) | async-done | bytes 262160 | tf_op jit(solution)/shard_map/reduce_scatter | solution.py:131
  708.9 1.9 reshape.112
  710.8 8.9 %all-to-all-start.1 = ((f32[8,4,4096]{2,1,0:T(4,128)}), f32[8,4,4096]{2,1,0:T(4,128)S(1)}, u32[]{:S(2)}, u32[]{:S(2)}) async-start(f32[8,4,4096]{2,1,0:T(4,128)} %reshape.112), calls=%async_computation.3 | async-start | bytes 1048576 | tf_op jit(solution)/shard_map/all_to_all | solution.py:137
  720.2 9.0 %all-to-all-done.1 = f32[8,4,4096]{2,1,0:T(4,128)S(1)} async-done(((f32[8,4,4096]{2,1,0:T(4,128)}), f32[8,4,4096]{2,1,0:T(4,128)S(1)}, u32[]{:S(2)}, u32[]{:S(2)}) %all-to-all-start.1) | async-done | bytes 524320 | tf_op jit(solution)/shard_map/all_to_all | solution.py:137
  (252 shorter events, 69.4 us)
Async XLA Ops:
  7.2 33.1 %copy-start = (bf16[256,1024]{1,0:T(8,128)(2,1)S(1)}, bf16[256,1024]{1,0:T(8,128)(2,1)}, u32[]{:S(2)}) copy-start(bf16[256,1024]{1,0:T(8,128)(2,1)} %param.28) | copy-start | bytes 1572868
  7.2 119.0 %all-gather.13.cloned.1.call-start = ((), (), s32[]{:S(2)}) async-start(), calls=%async_computation.9 | async-start | bytes 2162688 | tf_op jit(solution)/shard_map/all_gather | solution.py:15
  8.0 4.8 collective-permute-start
  43.2 265.9 %copy-start.4 = (bf16[64,1024]{1,0:T(8,128)(2,1)S(1)}, bf16[64,1024]{1,0:T(8,128)(2,1)}, u32[]{:S(2)}) copy-start(bf16[64,1024]{1,0:T(8,128)(2,1)} %param.23) | copy-start | bytes 393220
  43.2 265.9 %copy-start.6 = (f32[1024]{0:T(1024)S(1)}, f32[1024]{0:T(1024)}, u32[]{:S(2)}) copy-start(f32[1024]{0:T(1024)} %param.31) | copy-start | bytes 12292
  47.6 157.0 %all-gather.11.cloned.1.call-start = ((), (), s32[]{:S(2)}) async-start(), calls=%async_computation.8 | async-start | bytes 2162688 | tf_op jit(solution)/shard_map/all_gather | solution.py:15
  48.3 260.9 %all-gather.7.cloned.1.call-start = ((), (), s32[]{:S(2)}) async-start(), calls=%async_computation.4 | async-start | bytes 8650752 | tf_op jit(solution)/shard_map/all_gather | solution.py:98
  49.0 298.7 %reduce-scatter.3.cloned.1.call-start = ((), (), s32[]{:S(2)}) async-start(), calls=%async_computation.5 | async-start | bytes 1179648 | tf_op jit(solution)/shard_map/reduce_scatter | solution.py:101
  309.2 6.2 copy-start.8
  309.2 38.5 %copy-start.2 = (bf16[8,4096]{1,0:T(8,128)(2,1)S(1)}, bf16[8,4096]{1,0:T(8,128)(2,1)}, u32[]{:S(2)}) copy-start(bf16[8,4096]{1,0:T(8,128)(2,1)} %param.33) | copy-start | bytes 196612
  309.2 39.6 %copy-start.7 = (f32[4096]{0:T(1024)S(1)}, f32[4096]{0:T(1024)}, u32[]{:S(2)}) copy-start(f32[4096]{0:T(1024)} %param.34) | copy-start | bytes 49156
  315.3 145.7 %all-gather.9.cloned.1.call-start = ((), (), s32[]{:S(2)}) async-start(), calls=%async_computation.6 | async-start | bytes 8650752 | tf_op jit(solution)/shard_map/all_gather | solution.py:127
  363.1 345.9 %reduce-scatter.5.cloned.1.call-start = ((), (), s32[]{:S(2)}) async-start(), calls=%async_computation.7 | async-start | bytes 8650752 | tf_op jit(solution)/shard_map/reduce_scatter | solution.py:131
  486.0 233.6 %copy-start.5 = (f32[4096,8]{0,1:T(8,128)S(1)}, f32[4096,8]{0,1:T(8,128)}, u32[]{:S(2)}) copy-start(f32[4096,8]{0,1:T(8,128)} %param.35) | copy-start | bytes 393220
  486.1 244.5 %copy-start.1 = (f32[8,4096]{1,0:T(8,128)S(1)}, f32[8,4096]{1,0:T(8,128)}, u32[]{:S(2)}) copy-start(f32[8,4096]{1,0:T(8,128)} %reduce-scatter.3.cloned.1.call-done) | copy-start | bytes 393220
  710.8 18.3 %all-to-all-start.1 = ((f32[8,4,4096]{2,1,0:T(4,128)}), f32[8,4,4096]{2,1,0:T(4,128)S(1)}, u32[]{:S(2)}, u32[]{:S(2)}) async-start(f32[8,4,4096]{2,1,0:T(4,128)} %reshape.112), calls=%async_computation.3 | async-start | bytes 1048576 | tf_op jit(solution)/shard_map/all_to_all | solution.py:137
  730.6 0.7 copy-start.3
Sparse Core Ops, SparseCore 0:
  47.7 78.5 all-gather.12
  129.4 75.1 all-gather.10
  207.0 102.1 all-gather.6
  315.4 32.2 reduce-scatter.2
  363.2 97.7 all-gather.8
  486.2 222.6 reduce-scatter.4
where the time goes:
time: 743 us; the launch traced here: 738 us
  waiting for transfers between devices  521 us (70%)
  other arithmetic  103 us (14%)
  blocking collectives  35.9 us (5%)
  matrix products  34.8 us (5%)
  between operations  14.4 us (2%)
  starting transfers between devices  13.2 us (2%)
  local copies, waits for them, and re-layouts  13 us (2%)
    reduce_scatter x1, waiting for transfers between devices, body(): lax.psum_scatter(jnp.dot(activated, down_local, preferred_element_type=jn...  223 us
    all_gather x2, waiting for transfers between devices, entering(): everything = jax.tree.map(lambda part: lax.all_gather(part, axis), array)  155 us
    all_gather x1, waiting for transfers between devices, body(): shard_part = lax.all_gather(arrived, 'seq', axis=0, tiled=True)  97.7 us
    reduce_sum x64, other arithmetic, advance(): return (carried, jnp.sum(output_t[:, None] * carried, axis=0))  61.7 us
    reduce_scatter x1, waiting for transfers between devices, body(): lax.psum_scatter(partial_value, 'exp', scatter_dimension=0, tiled=True)  32 us
    select_n x32, other arithmetic, hop(): return jax.tree.map(lambda a, b: jnp.where(reached, a, b), new, before)  29.3 us
    psum x1, blocking collectives, body(): delta_sum, state_maps = lax.psum((delta_part, state_part), 'exp')  23.9 us
    dot_general x1, matrix products, body(): jnp.dot(activated, down_local, preferred_element_type=jnp.float32)  15.4 us
  transfers between devices with their start and end apart: 8, of which 7 were waited for; matrix products, arithmetic and copies ran while one was open for 14% of the time, Pallas kernels for 0%

commit v1 on v0

--- a/solution.py
+++ b/solution.py
@@ -2,6 +2,25 @@
 import jax.numpy as jnp
 from jax import lax
 from jax.sharding import PartitionSpec as P
+
+
+def enter_the_unit(raw, bus_axis):
+    view_out, block_last, v1 = (lax.axis_size(bus_axis), lax.axis_index(bus_axis), raw.shape[0])
+    outcome_arr, clean = (raw, 1)
+    while clean < view_out:
+        outcome_arr = jnp.concatenate(
+            [
+                outcome_arr,
+                lax.ppermute(
+                    outcome_arr,
+                    axis_name=bus_axis,
+                    perm=tuple(((jj, (jj - clean) % view_out) for jj in range(view_out))),
+                ),
+            ],
+            0,
+        )
+        clean = 2 * clean
+    return jnp.roll(outcome_arr, block_last * v1, 0)
 
 
 def shifted(block, axis, distance):
@@ -124,7 +143,7 @@
     gate_local = w_gate[0]
     up_local = w_up[0]
     down_local = w_down[0]
-    shard_part = lax.all_gather(arrived, "seq", axis=0, tiled=True)
+    shard_part = enter_the_unit(arrived, "seq")
     gate_part = jnp.dot(shard_part, gate_local, preferred_element_type=jnp.float32)
     up_part = jnp.dot(shard_part, up_local, preferred_element_type=jnp.float32)
     activated = (jax.nn.silu(gate_part) * up_part).astype(jnp.bfloat16)

time: 743 us -> 984 us (1.32)
  waiting for transfers between devices: 521 us -> 727 us
  local copies, waits for them, and re-layouts: 13 us -> 34.8 us
  starting transfers between devices: 13.2 us -> 28.4 us
    ppermute x0 -> x5, waiting for transfers between devices: none -> 275 us  [enter_the_unit(): lax.ppermute(outcome_arr, axis_name=bus_axis, perm=tuple(((jj, (jj - clea...]
    all_gather x1 -> x0, waiting for transfers between devices: 97.7 us -> none  [body(): shard_part = lax.all_gather(arrived, 'seq', axis=0, tiled=True)]
    reduce_scatter x1, waiting for transfers between devices: 223 us -> 255 us  [body(): lax.psum_scatter(jnp.dot(activated, down_local, preferred_element_type=jn...]
    ppermute x0 -> x5, starting transfers between devices: none -> 15.4 us  [enter_the_unit(): lax.ppermute(outcome_arr, axis_name=bus_axis, perm=tuple(((jj, (jj - clea...]
    unnamed x19 -> x37, local copies, waits for them, and re-layouts: 0.13 us -> 15.3 us
  transfers between devices with their start and end apart: 8 -> 12, of which waited for: 7 -> 11; matrix products, arithmetic and copies ran while one was open for 14% -> 11% of each run, Pallas kernels for 0% -> 0%
where the time goes in v1:
time: 984 us; the launch traced here: 979 us
  waiting for transfers between devices  727 us (74%)
  other arithmetic  103 us (10%)
  blocking collectives  35.9 us (4%)
  local copies, waits for them, and re-layouts  34.8 us (4%)
  matrix products  33.1 us (3%)
  starting transfers between devices  28.4 us (3%)
  between operations  14.1 us (1%)
    ppermute x5, waiting for transfers between devices, enter_the_unit(): lax.ppermute(outcome_arr, axis_name=bus_axis, perm=tuple(((jj, (jj - clea...  275 us
    reduce_scatter x1, waiting for transfers between devices, body(): lax.psum_scatter(jnp.dot(activated, down_local, preferred_element_type=jn...  255 us
    all_gather x2, waiting for transfers between devices, entering(): everything = jax.tree.map(lambda part: lax.all_gather(part, axis), array)  152 us
    reduce_sum x64, other arithmetic, advance(): return (carried, jnp.sum(output_t[:, None] * carried, axis=0))  61.6 us
    reduce_scatter x1, waiting for transfers between devices, body(): lax.psum_scatter(partial_value, 'exp', scatter_dimension=0, tiled=True)  32.4 us
    select_n x32, other arithmetic, hop(): return jax.tree.map(lambda a, b: jnp.where(reached, a, b), new, before)  29.3 us
    psum x1, blocking collectives, body(): delta_sum, state_maps = lax.psum((delta_part, state_part), 'exp')  23.9 us
  transfers between devices with their start and end apart: 12, of which 11 were waited for; matrix products, arithmetic and copies ran while one was open for 11% of the time, Pallas kernels for 0%

profile of v1, /device:TPU:1, one launch (start us, length us, event | category | flops | bytes accessed | tf_op | source)
XLA Modules:
  0.0 979.0 jit_solution(15519813588085259005)
XLA Ops:
  8.0 3.9 collective-permute-start
  12.8 1.5 multiply_convert_fusion.2
  14.3 1.0 fusion.43
  15.3 1.3 fusion.42
  16.5 23.9 %all-reduce = (bf16[64,256]{1,0:T(8,128)(2,1)S(1)}, f32[64,32]{0,1:T(8,128)S(1)}) all-reduce(f32[64,256]{1,0:T(8,128)S(1)} %fusion.42, f32[64,32]{0,1:T(8,128)S(1)} %fusion.43), channel_id=1, replica_groups=mesh['seq'=32,'exp'=8] {'exp'}, use_global_device_ids=true, to_apply=%region_0.1 | all-reduce | flops 18432 | bytes 114688 | tf_op jit(solution)/shard_map/psum | solution.py:85
  40.4 1.0 fusion.38
  41.7 1.5 fusion.40
  43.4 4.3 broadcast_multiply_fusion
  48.7 73.2 %all-gather.8.cloned.1.call-done = f32[512,1024]{1,0:T(8,128)} async-done(((f32[16,1024]{1,0:T(8,128)}), f32[512,1024]{1,0:T(8,128)}) %all-gather.8.cloned.1.call-update) | async-done | bytes 2097168 | tf_op jit(solution)/shard_map/all_gather | solution.py:34
  121.9 78.3 %all-gather.10.cloned.1.call-done = f32[512,1024]{1,0:T(8,128)} async-done(((f32[16,1024]{1,0:T(8,128)}), f32[512,1024]{1,0:T(8,128)}) %all-gather.10.cloned.1.call-update) | async-done | bytes 2097168 | tf_op jit(solution)/shard_map/all_gather | solution.py:34
  200.2 30.0 %while.29 = (s32[]{:T(128)}, f32[16,1024]{1,0:T(8,128)S(1)}, s32[]{:T(128)}, f32[32,16,1024]{2,1,0:T(8,128)}, f32[32,16,1024]{2,1,0:T(8,128)}) while((s32[]{:T(128)}, f32[16,1024]{1,0:T(8,128)S(1)}, s32[]{:T(128)}, f32[32,16,1024]{2,1,0:T(8,128)}, f32[32,16,1024]{2,1,0:T(8,128)}) %tuple.94), condition=%wide.region_5.6_spmd.clone.clone, body=%wide.region_4.5_spmd.clone.sunk.clone | while | flops 65540 | bytes 262237 | solution.py:46
  230.2 71.4 %while.28 = (s32[]{:T(128)}, f32[16,1024]{1,0:T(8,128)S(1)}, f32[64,1024]{1,0:T(8,128)S(1)}, f32[64,16,1024]{2,1,0:T(8,128)}, f32[64,16,1024]{2,1,0:T(8,128)}, /*index=5*/f32[64,16]{1,0:T(8,128)S(1)}) while((s32[]{:T(128)}, f32[16,1024]{1,0:T(8,128)S(1)}, f32[64,1024]{1,0:T(8,128)S(1)}, f32[64,16,1024]{2,1,0:T(8,128)}, ...), condition=%wide.region_8.9_spmd.clone, body=%wide.region_6.8_spmd.sunk.clone | while | flops 64514 | bytes 274713 | solution.py:111
  233.6 1.0 multiply_reduce_fusion.6
  255.9 1.0 multiply_reduce_fusion.6
  257.0 1.0 multiply_reduce_fusion.6
  258.1 1.0 multiply_reduce_fusion.6
  259.2 1.0 multiply_reduce_fusion.6
  260.3 1.0 multiply_reduce_fusion.6
  265.9 1.0 multiply_reduce_fusion.6
  267.0 1.0 multiply_reduce_fusion.6
  271.5 1.0 multiply_reduce_fusion.6
  272.6 1.0 multiply_reduce_fusion.6
  273.7 1.0 multiply_reduce_fusion.6
  274.9 1.0 multiply_reduce_fusion.6
  280.4 1.0 multiply_reduce_fusion.6
  281.6 1.0 multiply_reduce_fusion.6
  282.7 1.0 multiply_reduce_fusion.6
  284.9 1.0 multiply_reduce_fusion.6
  286.0 1.0 multiply_reduce_fusion.6
  287.1 1.0 multiply_reduce_fusion.6
  288.3 1.0 multiply_reduce_fusion.6
  289.4 1.0 multiply_reduce_fusion.6
  293.8 1.0 multiply_reduce_fusion.6
  295.0 1.0 multiply_reduce_fusion.6
  301.6 2.9 all-gather.6.cloned.1.call-done
  304.6 6.1 fusion.18
  311.1 32.4 %reduce-scatter.3.cloned.1.call-done = f32[8,4096]{1,0:T(8,128)} async-done(((f32[64,4096]{1,0:T(8,128)}), f32[8,4096]{1,0:T(8,128)}) %reduce-scatter.3.cloned.1.call-update) | async-done | bytes 131088 | tf_op jit(solution)/shard_map/reduce_scatter | solution.py:120
  343.6 1.1 multiply_reduce_fusion.3
  344.6 1.0 multiply_convert_fusion.3
  346.1 12.1 %all_to_all.28 = bf16[8,4,4096]{2,1,0:T(4,128)(2,1)S(1)} all-to-all(bf16[8,4,4096]{2,1,0:T(4,128)(2,1)S(1)} %all_to_all.18), channel_id=1, replica_groups=mesh['seq'=32,'exp'=8] {'exp'}, dimensions={0} | all-to-all | bytes 524288 | tf_op jit(solution)/shard_map/all_to_all | solution.py:142
  358.2 5.2 collective-permute-start.1
  363.4 4.6 collective-permute-done.1
  368.0 2.6 collective-permute-start.2
  370.6 10.5 %collective-permute-done.2 = bf16[64,4096]{1,0:T(8,128)(2,1)S(1)} collective-permute-done((bf16[64,4096]{1,0:T(8,128)(2,1)S(1)}, bf16[64,4096]{1,0:T(8,128)(2,1)S(1)}, u32[]{:S(2)}, u32[]{:S(2)}) %collective-permute-start.2) | collective-permute-done | bytes 524320 | tf_op jit(solution)/shard_map/ppermute | solution.py:14
  381.1 1.2 collective-permute-start.3
  382.3 20.7 %collective-permute-done.3 = bf16[128,4096]{1,0:T(8,128)(2,1)S(1)} collective-permute-done((bf16[128,4096]{1,0:T(8,128)(2,1)S(1)}, bf16[128,4096]{1,0:T(8,128)(2,1)S(1)}, u32[]{:S(2)}, u32[]{:S(2)}) %collective-permute-start.3) | collective-permute-done | bytes 1048608 | tf_op jit(solution)/shard_map/ppermute | solution.py:14
  403.2 2.0 collective-permute-start.4
  406.8 1.1 constant_dynamic-update-slice_fusion.2
  407.9 1.6 constant_dynamic-update-slice_fusion.1
  409.5 57.9 %collective-permute-done.4 = bf16[256,4096]{1,0:T(8,128)(2,1)S(1)} collective-permute-done((bf16[256,4096]{1,0:T(8,128)(2,1)S(1)}, bf16[256,4096]{1,0:T(8,128)(2,1)S(1)}, u32[]{:S(2)}, u32[]{:S(2)}) %collective-permute-start.4) | collective-permute-done | bytes 2097184 | tf_op jit(solution)/shard_map/ppermute | solution.py:14
  467.4 1.4 copy-done.2
  468.8 2.5 constant_dynamic-update-slice_fusion
  471.3 4.5 collective-permute-start.5
  475.8 181.5 %collective-permute-done.5 = bf16[512,4096]{1,0:T(8,128)(2,1)} collective-permute-done((bf16[512,4096]{1,0:T(8,128)(2,1)}, bf16[512,4096]{1,0:T(8,128)(2,1)}, u32[]{:S(2)}, u32[]{:S(2)}) %collective-permute-start.5) | collective-permute-done | bytes 4194336 | tf_op jit(solution)/shard_map/ppermute | solution.py:14
  657.3 4.7 constant_dynamic-update-slice_fusion.11
  664.3 1.1 constant_dynamic-update-slice_fusion.7
  665.4 1.5 constant_dynamic-update-slice_fusion.6
  666.8 4.8 constant_dynamic-update-slice_fusion.5
  671.6 7.7 fusion.2
  679.3 15.6 %convolution_convert_fusion = bf16[1024,4096]{1,0:T(8,128)(2,1)} fusion(bf16[1,448,4096]{2,1,0:T(8,128)(2,1)} %param.38, f32[1024,448]{0,1:T(8,128)} %fusion.2, bf16[2048,4096]{1,0:T(8,128)(2,1)} %constant_dynamic-update-slice_fusion.5, s32[]{:T(128)S(6)} %select_n.64, bf16[1,4096,448]{1,2,0:T(8,128)(2,1)} %param.36), kind=kOutput, calls=%fused_computation.9 | convolution fusion | flops 7523139584 | bytes 25952260 | tf_op jit(solution)/shard_map/dot_general | solution.py:151
  695.2 255.0 %reduce-scatter.5.cloned.1.call-done = bf16[32,4096]{1,0:T(8,128)(2,1)} async-done(((bf16[1024,4096]{1,0:T(8,128)(2,1)}), bf16[32,4096]{1,0:T(8,128)(2,1)}) %reduce-scatter.5.cloned.1.call-update) | async-done | bytes 262160 | tf_op jit(solution)/shard_map/reduce_scatter | solution.py:150
  950.2 1.9 reshape.112
  952.1 8.8 all-to-all-start.1
  961.4 9.0 all-to-all-done.1
  (282 shorter events, 88.3 us)
Async XLA Ops:
  7.2 33.3 %copy-start = (bf16[256,1024]{1,0:T(8,128)(2,1)S(1)}, bf16[256,1024]{1,0:T(8,128)(2,1)}, u32[]{:S(2)}) copy-start(bf16[256,1024]{1,0:T(8,128)(2,1)} %param.28) | copy-start | bytes 1572868
  7.2 114.7 %all-gather.8.cloned.1.call-start = ((), (), s32[]{:S(2)}) async-start(), calls=%async_computation.7 | async-start | bytes 2162688 | tf_op jit(solution)/shard_map/all_gather | solution.py:34
  8.0 4.8 collective-permute-start
  43.2 157.0 %all-gather.10.cloned.1.call-start = ((), (), s32[]{:S(2)}) async-start(), calls=%async_computation.8 | async-start | bytes 2162688 | tf_op jit(solution)/shard_map/all_gather | solution.py:34
  43.4 261.2 %copy-start.7 = (bf16[64,1024]{1,0:T(8,128)(2,1)S(1)}, bf16[64,1024]{1,0:T(8,128)(2,1)}, u32[]{:S(2)}) copy-start(bf16[64,1024]{1,0:T(8,128)(2,1)} %param.23) | copy-start | bytes 393220
  43.4 261.1 %copy-start.9 = (f32[1024]{0:T(1024)S(1)}, f32[1024]{0:T(1024)}, u32[]{:S(2)}) copy-start(f32[1024]{0:T(1024)} %param.31) | copy-start | bytes 12292
  47.8 256.8 %all-gather.6.cloned.1.call-start = ((), (), s32[]{:S(2)}) async-start(), calls=%async_computation.4 | async-start | bytes 8650752 | tf_op jit(solution)/shard_map/all_gather | solution.py:117
  48.5 295.0 %reduce-scatter.3.cloned.1.call-start = ((), (), s32[]{:S(2)}) async-start(), calls=%async_computation.5 | async-start | bytes 1179648 | tf_op jit(solution)/shard_map/reduce_scatter | solution.py:120
  304.6 6.2 copy-start.11
  304.6 39.0 %copy-start.5 = (bf16[8,4096]{1,0:T(8,128)(2,1)S(1)}, bf16[8,4096]{1,0:T(8,128)(2,1)}, u32[]{:S(2)}) copy-start(bf16[8,4096]{1,0:T(8,128)(2,1)} %param.33) | copy-start | bytes 196612
  304.6 40.0 %copy-start.10 = (f32[4096]{0:T(1024)S(1)}, f32[4096]{0:T(1024)}, u32[]{:S(2)}) copy-start(f32[4096]{0:T(1024)} %param.34) | copy-start | bytes 49156
  310.7 639.5 %reduce-scatter.5.cloned.1.call-start = ((), (), s32[]{:S(2)}) async-start(), calls=%async_computation.6 | async-start | bytes 8650752 | tf_op jit(solution)/shard_map/reduce_scatter | solution.py:150
  358.2 9.8 collective-permute-start.1
  368.0 13.0 %collective-permute-start.2 = (bf16[64,4096]{1,0:T(8,128)(2,1)S(1)}, bf16[64,4096]{1,0:T(8,128)(2,1)S(1)}, u32[]{:S(2)}, u32[]{:S(2)}) collective-permute-start(bf16[64,4096]{1,0:T(8,128)(2,1)S(1)} %pad_maximum_fusion.2), channel_id=1, source_target_pairs={{0,240},{8,248},{16,0},{24,8},{32,16},{40,24},{48,32},{56,40},{64,... | collective-permute-start | bytes 1572872 | tf_op jit(solution)/shard_map/ppermute | solution.py:14
  381.1 21.8 %collective-permute-start.3 = (bf16[128,4096]{1,0:T(8,128)(2,1)S(1)}, bf16[128,4096]{1,0:T(8,128)(2,1)S(1)}, u32[]{:S(2)}, u32[]{:S(2)}) collective-permute-start(bf16[128,4096]{1,0:T(8,128)(2,1)S(1)} %pad_maximum_fusion.1), channel_id=1, source_target_pairs={{0,224},{8,232},{16,240},{24,248},{32,0},{40,8},{48,16},{56,24},{6... | collective-permute-start | bytes 3145736 | tf_op jit(solution)/shard_map/ppermute | solution.py:14
  403.2 64.2 %collective-permute-start.4 = (bf16[256,4096]{1,0:T(8,128)(2,1)S(1)}, bf16[256,4096]{1,0:T(8,128)(2,1)S(1)}, u32[]{:S(2)}, u32[]{:S(2)}) collective-permute-start(bf16[256,4096]{1,0:T(8,128)(2,1)S(1)} %pad_maximum_fusion), channel_id=1, source_target_pairs={{0,192},{8,200},{16,208},{24,216},{32,224},{40,232},{48,240},{56,2... | collective-permute-start | bytes 6291464 | tf_op jit(solution)/shard_map/ppermute | solution.py:14
  467.4 1.4 copy-start.2
  471.3 186.0 %collective-permute-start.5 = (bf16[512,4096]{1,0:T(8,128)(2,1)}, bf16[512,4096]{1,0:T(8,128)(2,1)}, u32[]{:S(2)}, u32[]{:S(2)}) collective-permute-start(bf16[512,4096]{1,0:T(8,128)(2,1)} %get-tuple-element.192), channel_id=1, source_target_pairs={{0,128},{8,136},{16,144},{24,152},{32,160},{40,168},{48,176},{56,1... | collective-permute-start | bytes 12582920 | tf_op jit(solution)/shard_map/ppermute | solution.py:14
  662.0 3.4 copy-start.3
  666.8 4.8 copy-start.12
  694.9 266.0 %copy-start.8 = (f32[4096,8]{0,1:T(8,128)S(1)}, f32[4096,8]{0,1:T(8,128)}, u32[]{:S(2)}) copy-start(f32[4096,8]{0,1:T(8,128)} %param.35) | copy-start | bytes 393220
  695.0 276.9 %copy-start.4 = (f32[8,4096]{1,0:T(8,128)S(1)}, f32[8,4096]{1,0:T(8,128)}, u32[]{:S(2)}) copy-start(f32[8,4096]{1,0:T(8,128)} %reduce-scatter.3.cloned.1.call-done) | copy-start | bytes 393220
  695.0 277.5 %copy-start.1 = (bf16[256,1024]{1,0:T(8,128)(2,1)S(1)}, bf16[256,1024]{1,0:T(8,128)(2,1)}, u32[]{:S(2)}) copy-start(bf16[256,1024]{1,0:T(8,128)(2,1)} %param.28) | copy-start | bytes 1572868
  952.1 18.3 %all-to-all-start.1 = ((f32[8,4,4096]{2,1,0:T(4,128)}), f32[8,4,4096]{2,1,0:T(4,128)S(1)}, u32[]{:S(2)}, u32[]{:S(2)}) async-start(f32[8,4,4096]{2,1,0:T(4,128)} %reshape.112), calls=%async_computation.3 | async-start | bytes 1048576 | tf_op jit(solution)/shard_map/all_to_all | solution.py:156
  971.8 0.7 copy-start.6
Sparse Core Ops, SparseCore 0:
  43.4 78.4 all-gather.7
  125.1 75.1 all-gather.9
  202.7 101.8 all-gather.5
  310.8 32.6 reduce-scatter.2
  695.1 255.0 reduce-scatter.4
